TPU v7x, 32 devices: a whole 2x2x4 slice. The times are simulated.
32 devices in a mesh: rep: 2 (over y), ctx: 16 (over z, x, core).
Axes of the slice: x: 2, y: 2, z: 4, core: 2. Of those that a mesh axis runs over, the one named last changes fastest.
Arguments:
- resid: bfloat16 [512, 8192], P('rep', 'ctx'), parts along dimension 0, may hold values from -6 to 6
- prefix_values: bfloat16 [4096, 8192], P(('rep', 'ctx')), parts along dimension 0, may hold values from -6 to 6
- tail_values: bfloat16 [32, 48, 8192], P('rep', None, 'ctx'), parts along dimension 0, may hold values from -6 to 6
- tail_lengths: int32 [32], P('rep'), parts along dimension 0, may hold values from 0 to 48, as said below
- norm_gain: float32 [8192], replicated, may hold values from 0.1 to 1.9
- in_weight: bfloat16 [3, 8192, 8192], P(None, None, 'ctx'), may hold values from -0.0625 to 0.0625
- skip_gain: float32 [8192], replicated, may hold values from -1 to 1
- mode_residues: float32 [8, 8192], replicated, may hold values from -4 to 4
- mode_rates: float32 [8, 8192], replicated, may hold values from 0.000118371216 to 0.1
- out_weight: bfloat16 [8192, 8192], P(None, 'ctx'), may hold values from -0.0625 to 0.0625
- mlp_gain: float32 [8192], replicated, may hold values from 0.1 to 1.9
- gate_weight: bfloat16 [8192, 16384], P(None, 'ctx'), may hold values from -0.0625 to 0.0625
- up_weight: bfloat16 [8192, 16384], P(None, 'ctx'), may hold values from -0.0625 to 0.0625
- down_weight: bfloat16 [16384, 8192], P('ctx'), may hold values from -0.046875 to 0.046875
Outputs:
- output: bfloat16 [512, 8192], P(('rep', 'ctx')), parts along dimension 0
There are 2 independent parts, one for each index of `rep`. A program takes and returns all parts, laid end to end along the dimension named above; an argument that names none is the same for every part. Nothing has to cross between parts.
Inputs may be any that keep to these rules, and one draw needn't show every extreme that they name: `tail_lengths`: at least one continuation has all 48 tail slots live.
All inputs are finite; a program needn't handle non-finite values.
Results may differ from a plain program's by a relative error of at most 0.012.
Values may be sent and summed in bfloat16 or wider, within the bound.
A program may use at most 192 MiB of HBM per device.

v0:
```python
import jax
import jax.numpy as jnp
from jax import lax
from jax.sharding import PartitionSpec as P

D = 8192
W = 16


def rms_scale(values, gain):
    values = values.astype(jnp.float32)
    inverse = lax.rsqrt(jnp.mean(values * values, axis=-1, keepdims=True) + 1e-05)
    return (values * inverse * gain).astype(jnp.bfloat16)


def filter_taps(residues, rates, length):
    lags = jnp.arange(length).astype(jnp.float32)
    weights = residues * jnp.sqrt(rates)
    result = jnp.zeros((length, residues.shape[1]), jnp.float32)
    for mode in range(residues.shape[0]):
        result = result + weights[mode][None, :] * jnp.exp(-rates[mode][None, :] * lags[:, None])
    return result


def lag_toeplitz(near_taps, tail_slots, window):
    positions = tail_slots + window
    row_pos = jnp.arange(window)[:, None, None]
    col_pos = jnp.arange(positions)[None, :, None]
    lag_pos = jnp.arange(positions)[None, None, :]
    picked = (lag_pos == tail_slots + row_pos - col_pos) & (col_pos <= tail_slots + row_pos)
    return jnp.einsum("jpn,nc->jpc", picked.astype(jnp.float32), near_taps)


def mode_states(values, distance, rates):
    stacked = []
    for mode in range(rates.shape[0]):
        stacked.append(jnp.sum(jnp.exp(-rates[mode][None, :] * distance[:, None]) * values, axis=0))
    return jnp.stack(stacked)


def expand_states(states, residues, rates, window):
    lags = jnp.arange(window).astype(jnp.float32)
    weights = residues * jnp.sqrt(rates) * states
    result = jnp.zeros((window, states.shape[1]), jnp.float32)
    for mode in range(states.shape[0]):
        result = result + weights[mode][None, :] * jnp.exp(-rates[mode][None, :] * lags[:, None])
    return result


def on_device(
    resid,
    prefix_values,
    tail_values,
    tail_lengths,
    norm_gain,
    in_weight,
    skip_gain,
    mode_residues,
    mode_rates,
    out_weight,
    mlp_gain,
    gate_weight,
    up_weight,
    down_weight,
):
    devices = lax.axis_size("ctx")
    my_index = lax.axis_index("ctx")
    own_width = resid.shape[1]
    row_count = resid.shape[0]
    prompt_rows = prefix_values.shape[0]
    tail_slots = tail_values.shape[1]
    branch_count = tail_values.shape[0]
    first_col = my_index * own_width
    gathered = lax.all_gather(resid, "ctx", axis=1, tiled=True)
    normed = rms_scale(gathered, norm_gain)
    first_gate = jnp.dot(normed, in_weight[0], preferred_element_type=jnp.float32)
    out_gate = jnp.dot(normed, in_weight[1], preferred_element_type=jnp.float32)
    value_proj = jnp.dot(normed, in_weight[2], preferred_element_type=jnp.float32)
    window_value = first_gate * value_proj
    prompt_total = prompt_rows * devices
    distance = (
        prompt_total + tail_slots - (my_index * prompt_rows + jnp.arange(prompt_rows))
    ).astype(jnp.float32)
    states = mode_states(prefix_values, distance, mode_rates)
    residues_own = lax.dynamic_slice_in_dim(mode_residues, first_col, own_width, 1)
    rates_own = lax.dynamic_slice_in_dim(mode_rates, first_col, own_width, 1)
    own_states = lax.psum_scatter(states, "ctx", scatter_dimension=1, tiled=True)
    prefix_part = expand_states(own_states, residues_own, rates_own, W)
    near_taps = filter_taps(residues_own, rates_own, tail_slots + W)
    toeplitz = lag_toeplitz(near_taps, tail_slots, W)
    live = jnp.arange(tail_slots)[None, :] < tail_lengths[:, None]
    tail_live = jnp.where(live[:, :, None], tail_values.astype(jnp.float32), 0.0)
    window_rows = window_value.reshape(branch_count, W, own_width)
    branch_values = jnp.concatenate([tail_live, window_rows], axis=1)
    branch_conv = jnp.einsum("jpc,bpc->bjc", toeplitz, branch_values)
    skip_own = lax.dynamic_slice_in_dim(skip_gain, first_col, own_width)
    combined = out_gate.reshape(branch_count, W, own_width) * (
        branch_conv + prefix_part[None] + skip_own * window_rows
    )
    mixer_in = combined.reshape(row_count, own_width).astype(jnp.bfloat16)
    mixed = resid.astype(jnp.float32) + jnp.dot(
        lax.all_gather(mixer_in, "ctx", axis=1, tiled=True),
        out_weight,
        preferred_element_type=jnp.float32,
    )
    mixed_squares = lax.psum(jnp.sum(mixed * mixed, axis=1), "ctx")
    mixed_inverse = lax.rsqrt(mixed_squares / D + 1e-05)
    mlp_gain_own = lax.dynamic_slice_in_dim(mlp_gain, first_col, own_width)
    normed_mlp = (mixed * mixed_inverse[:, None] * mlp_gain_own[None, :]).astype(jnp.bfloat16)
    portion = lax.all_gather(normed_mlp, "ctx", axis=1, tiled=True)
    gate = jnp.dot(portion, gate_weight, preferred_element_type=jnp.float32)
    up_part = jnp.dot(portion, up_weight, preferred_element_type=jnp.float32)
    hidden = (jax.nn.silu(gate) * up_part).astype(jnp.bfloat16)
    product = jnp.dot(hidden, down_weight, preferred_element_type=jnp.float32)
    own_cols = lax.dynamic_slice_in_dim(product, first_col, own_width, 1) + mixed
    total = lax.psum_scatter(
        lax.dynamic_update_slice_in_dim(product, own_cols, first_col, 1),
        "ctx",
        scatter_dimension=0,
        tiled=True,
    )
    return total.astype(jnp.bfloat16)


def solution(mesh):
    return jax.shard_map(
        on_device,
        mesh=mesh,
        in_specs=(
            P("rep", "ctx"),
            P(("rep", "ctx"), None),
            P("rep", None, "ctx"),
            P("rep"),
            P(),
            P(None, None, "ctx"),
            P(),
            P(),
            P(),
            P(None, "ctx"),
            P(),
            P(None, "ctx"),
            P(None, "ctx"),
            P("ctx", None),
        ),
        out_specs=P(("rep", "ctx"), None),
        check_vma=False,
    )
```

profile of v0, /device:TPU:0, one launch (start us, length us, event | category | flops | bytes accessed | tf_op | source)
XLA Modules:
  0.0 454.7 jit_solution(12085558687546584423)
XLA Ops:
  6.5 2.7 slice_negate_fusion.7
  9.3 0.0 copy-start.6
  9.3 7.6 %fusion.19 = (f32[8192]{0:T(1024)S(1)}, f32[8192]{0:T(1024)S(1)}, f32[8192]{0:T(1024)S(1)}, f32[8192]{0:T(1024)S(1)}, f32[8192]{0:T(1024)S(1)}, /*index=5*/f32[8192]{0:T(1024)S(1)}, f32[8192]{0:T(1024)S(1)}, f32[8192]{0:T(1024)S(1)}) fusion(bf16[128,8192]{1,0:T(8,128)(2,1)} %param.15, f32[8192]{0:T(1024)S(1)} %bitcast.89, f32[128]{0:T(128)S(1)} %subtract_convert_fusion, ...), kind=kLoop, calls=%fused_computation.29 | loop fusion | flops 26148864 | bytes 2621952 | tf_op jit(solution)/shard_map/reduce_sum | solution.py:37
  16.9 1.1 stack.35
  18.0 0.0 reduce-scatter.3.cloned.1.call-update
  18.0 0.0 all-gather.4.cloned.1.call-start
  18.1 0.7 all-gather.4.cloned.1.call-update
  18.8 0.2 all-gather.6.cloned.1.call-start
  19.0 2.0 copy.15
  21.0 0.8 dynamic_slice.17
  21.8 1.1 dynamic-slice_negate_fusion.7
  22.9 0.1 iota_compare_fusion.1
  23.0 0.1 iota_compare_fusion.2
  23.1 0.1 iota_subtract_fusion
  23.2 1.8 convert_select_fusion
  25.0 51.2 %reduce-scatter.3.cloned.1.call-done = f32[8,512]{1,0:T(8,128)} async-done(((f32[8,8192]{1,0:T(8,128)}), f32[8,512]{1,0:T(8,128)}) %reduce-scatter.3.cloned.1.call-update) | async-done | bytes 16400 | tf_op jit(solution)/shard_map/reduce_scatter | solution.py:87
  76.2 0.8 fusion.92
  77.0 0.0 copy-start.5
  77.0 0.7 fusion.36
  77.7 2.8 copy.18
  80.5 0.1 multiply_add_fusion
  80.6 50.0 %all-gather.4.cloned.1.call-done = bf16[256,8192]{1,0:T(8,128)(2,1)} async-done(((bf16[256,512]{1,0:T(8,128)(2,1)}), bf16[256,8192]{1,0:T(8,128)(2,1)}) %all-gather.4.cloned.1.call-update) | async-done | bytes 4194320 | tf_op jit(solution)/shard_map/all_gather | solution.py:74
  130.6 3.3 fusion
  133.9 0.2 copy-done
  134.1 1.2 fusion.2
  135.3 7.3 %fusion.3 = f32[256,512]{1,0:T(8,128)S(1)} fusion(bf16[256,8192]{1,0:T(8,128)(2,1)S(1)} %fusion.2, bf16[3,8192,512]{2,1,0:T(8,128)(2,1)} %param.19), kind=kOutput, calls=%fused_computation.13 | convolution fusion | flops 2147483648 | bytes 13107200 | tf_op jit(solution)/shard_map/dot_general | solution.py:78
  142.6 5.8 %fusion.25 = f32[256,512]{1,0:T(8,128)S(1)} fusion(f32[256,512]{1,0:T(8,128)S(1)} %fusion.3, bf16[256,8192]{1,0:T(8,128)(2,1)S(1)} %fusion.2, bf16[3,8192,512]{2,1,0:T(8,128)(2,1)} %param.19), kind=kOutput, calls=%fused_computation.37 | convolution fusion | flops 2147614720 | bytes 13631488 | tf_op jit(solution)/shard_map/dot_general | solution.py:76
  148.4 2.7 copy.16
  151.1 5.5 %fusion.20 = f32[512,16,16]{2,1,0:T(8,128)} fusion(bf16[16,64,512]{1,0,2:T(8,128)(2,1)} %copy.18, bf16[16,16,512]{1,0,2:T(8,128)(2,1)S(1)} %copy.16, bf16[16,48,512]{1,0,2:T(8,128)(2,1)} %convert_select_fusion), kind=kOutput, calls=%fused_computation.30 | convolution fusion | flops 18874368 | bytes 2621440 | tf_op jit(solution)/shard_map/jpc,bpc->bjc/dot_general | solution.py:95
  156.6 2.8 copy.17
  159.4 0.0 copy-start.4
  159.4 7.7 %fusion.31 = bf16[16,16,512]{2,1,0:T(8,128)(2,1)} fusion(bf16[16,16,8192]{2,1,0:T(8,128)(2,1)} %bitcast.79, bf16[3,8192,512]{2,1,0:T(8,128)(2,1)} %param.19, f32[512,16,16]{0,2,1:T(8,128)S(1)} %copy.17, f32[16,16,512]{2,1,0:T(8,128)S(1)} %bitcast.81, f32[512]{0:T(512)S(1)} %dynamic_slice.17, f32[16,512]{1,0:T(8,128)S(1)} %multiply_add_fusion), kind=kOutput, calls=%fused_computation.40 | convolution fusion | flops 2148139008 | bytes 13928448 | tf_op jit(solution)/shard_map/dot_general | solution.py:77
  167.1 0.0 all-gather.6.cloned.1.call-update
  167.1 0.3 all-gather.8.cloned.1.call-start
  167.4 0.8 dynamic_slice.18
  168.2 50.5 %all-gather.6.cloned.1.call-done = bf16[256,8192]{1,0:T(8,128)(2,1)} async-done(((bf16[256,512]{1,0:T(8,128)(2,1)}), bf16[256,8192]{1,0:T(8,128)(2,1)}) %all-gather.6.cloned.1.call-update) | async-done | bytes 4194320 | tf_op jit(solution)/shard_map/all_gather | solution.py:102
  218.7 7.1 %multiply_reduce_fusion = (f32[256]{0:T(256)S(1)}, f32[256,512]{1,0:T(8,128)S(1)}) fusion(bf16[256,8192]{1,0:T(8,128)(2,1)} %all-gather.6.cloned.1.call-done, bf16[8192,512]{1,0:T(8,128)(2,1)} %param.23, bf16[256,512]{1,0:T(8,128)(2,1)S(1)} %copy-done.4), kind=kOutput, calls=%fused_computation.45 | convolution fusion | flops 2148007680 | bytes 13370368 | tf_op jit(solution)/shard_map/dot_general | solution.py:101
  225.7 30.9 %psum.7 = f32[256]{0:T(256)S(1)} all-reduce(f32[256]{0:T(256)S(1)} %get-tuple-element.47), channel_id=1, replica_groups=mesh['rep'=2,'ctx'=16] {'ctx'}, use_global_device_ids=true, to_apply=%region_11.12 | all-reduce | flops 256 | bytes 2048 | tf_op jit(solution)/shard_map/psum | solution.py:106
  256.7 0.8 multiply_convert_fusion
  257.5 0.0 all-gather.8.cloned.1.call-update
  257.5 0.0 reduce-scatter.5.cloned.1.call-start
  257.6 50.4 %all-gather.8.cloned.1.call-done = bf16[256,8192]{1,0:T(8,128)(2,1)} async-done(((bf16[256,512]{1,0:T(8,128)(2,1)}), bf16[256,8192]{1,0:T(8,128)(2,1)}) %all-gather.8.cloned.1.call-update) | async-done | bytes 4194320 | tf_op jit(solution)/shard_map/all_gather | solution.py:110
  308.0 9.4 %fusion.95 = f32[256,1024]{1,0:T(8,128)S(1)} fusion(bf16[256,8192]{1,0:T(8,128)(2,1)} %all-gather.8.cloned.1.call-done, bf16[8192,1024]{1,0:T(8,128)(2,1)} %param.25), kind=kOutput, calls=%fused_computation.133 | convolution fusion | flops 4294967296 | bytes 22020096 | tf_op jit(solution)/shard_map/dot_general | solution.py:111
  317.4 23.9 %fusion.38 = f32[256,8192]{1,0:T(8,128)} fusion(bf16[1024,8192]{1,0:T(8,128)(2,1)} %param.27, bf16[256,8192]{1,0:T(8,128)(2,1)} %all-gather.8.cloned.1.call-done, bf16[8192,1024]{1,0:T(8,128)(2,1)} %param.26, f32[256,1024]{1,0:T(8,128)S(1)} %fusion.95), kind=kOutput, calls=%fused_computation.49 | convolution fusion | flops 8591507456 | bytes 47185920 | tf_op jit(solution)/shard_map/dot_general | solution.py:114
  341.3 2.1 add_dynamic-update-slice_fusion
  343.5 0.0 reduce-scatter.5.cloned.1.call-update
  343.5 102.9 %reduce-scatter.5.cloned.1.call-done = f32[16,8192]{1,0:T(8,128)} async-done(((f32[256,8192]{1,0:T(8,128)}), f32[16,8192]{1,0:T(8,128)}) %reduce-scatter.5.cloned.1.call-update) | async-done | bytes 524304 | tf_op jit(solution)/shard_map/reduce_scatter | solution.py:116
  446.4 1.8 convert_element_type.99
  (18 shorter events, 0.1 us)
Async XLA Ops:
  6.5 69.6 %reduce-scatter.3.cloned.1.call-start = ((), (), s32[]{:S(2)}) async-start(), calls=%async_computation.3 | async-start | bytes 278528 | tf_op jit(solution)/shard_map/reduce_scatter | solution.py:87
  9.3 9.7 %copy-start.3 = (bf16[16,48,512]{2,1,0:T(8,128)(2,1)S(1)}, bf16[16,48,512]{2,1,0:T(8,128)(2,1)}, u32[]{:S(2)}) copy-start(bf16[16,48,512]{2,1,0:T(8,128)(2,1)} %param.16) | copy-start | bytes 2359300
  9.3 13.7 %copy-start.6 = (s32[16]{0:T(128)S(1)}, s32[16]{0:T(128)}, u32[]{:S(2)}) copy-start(s32[16]{0:T(128)} %param.17) | copy-start | bytes 196
  18.0 112.6 %all-gather.4.cloned.1.call-start = ((), (), s32[]{:S(2)}) async-start(), calls=%async_computation.2 | async-start | bytes 4456448 | tf_op jit(solution)/shard_map/all_gather | solution.py:74
  18.8 199.9 %all-gather.6.cloned.1.call-start = ((), (), s32[]{:S(2)}) async-start(), calls=%async_computation.4 | async-start | bytes 4456448 | tf_op jit(solution)/shard_map/all_gather | solution.py:102
  77.0 56.9 %copy-start.5 = (f32[8192]{0:T(1024)S(1)}, f32[8192]{0:T(1024)}, u32[]{:S(2)}) copy-start(f32[8192]{0:T(1024)} %param.18) | copy-start | bytes 98308
  130.6 3.4 copy-start
  135.3 7.3 %copy-start.1 = (bf16[256,8192]{1,0:T(8,128)(2,1)}, bf16[256,8192]{1,0:T(8,128)(2,1)S(1)}, u32[]{:S(2)}) copy-start(bf16[256,8192]{1,0:T(8,128)(2,1)S(1)} %fusion.2) | copy-start | bytes 12582916
  159.4 59.3 %copy-start.4 = (bf16[256,512]{1,0:T(8,128)(2,1)S(1)}, bf16[256,512]{1,0:T(8,128)(2,1)}, u32[]{:S(2)}) copy-start(bf16[256,512]{1,0:T(8,128)(2,1)} %param.14) | copy-start | bytes 786436
  167.1 140.9 %all-gather.8.cloned.1.call-start = ((), (), s32[]{:S(2)}) async-start(), calls=%async_computation.5 | async-start | bytes 4456448 | tf_op jit(solution)/shard_map/all_gather | solution.py:110
  225.7 91.7 %copy-start.2 = (f32[256,512]{1,0:T(8,128)}, f32[256,512]{1,0:T(8,128)S(1)}, u32[]{:S(2)}) copy-start(f32[256,512]{1,0:T(8,128)S(1)} %get-tuple-element.48) | copy-start | bytes 1572868
  257.5 188.9 %reduce-scatter.5.cloned.1.call-start = ((), (), s32[]{:S(2)}) async-start(), calls=%async_computation.6 | async-start | bytes 8912896 | tf_op jit(solution)/shard_map/reduce_scatter | solution.py:116
Sparse Core Ops, SparseCore 0:
  18.1 57.9 reduce-scatter.2
  78.3 52.2 all-gather.3
  167.2 51.3 all-gather.5
  257.6 50.2 all-gather.7
  343.6 102.7 reduce-scatter.4
where the time goes:
time: 455 us
  waiting for transfers between devices  306 us (67%)
  matrix products  67.4 us (15%)
  blocking collectives  30.9 us (7%)
  other arithmetic  23.5 us (5%)
  between operations  13.3 us (3%)
  local copies, waits for them, and re-layouts  13.1 us (3%)
    reduce_scatter x1, waiting for transfers between devices, on_device(): lax.psum_scatter(lax.dynamic_update_slice_in_dim(product, own_cols, first...  103 us
    reduce_scatter x1, waiting for transfers between devices, on_device(): lax.psum_scatter(states, 'ctx', scatter_dimension=1, tiled=True)  51.2 us
    all_gather x1, waiting for transfers between devices, on_device(): lax.all_gather(mixer_in, 'ctx', axis=1, tiled=True)  50.5 us
    all_gather x1, waiting for transfers between devices, on_device(): portion = lax.all_gather(normed_mlp, 'ctx', axis=1, tiled=True)  50.4 us
    all_gather x1, waiting for transfers between devices, on_device(): gathered = lax.all_gather(resid, 'ctx', axis=1, tiled=True)  50 us
    psum x1, blocking collectives, on_device(): mixed_squares = lax.psum(jnp.sum(mixed * mixed, axis=1), 'ctx')  30.9 us
    dot_general x1, matrix products, on_device(): product = jnp.dot(hidden, down_weight, preferred_element_type=jnp.float32)  23.9 us
    dot_general x1, matrix products, on_device(): gate = jnp.dot(portion, gate_weight, preferred_element_type=jnp.float32)  9.43 us
  transfers between devices with their start and end apart: 5, of which 5 were waited for; matrix products, arithmetic and copies ran while one was open for 2% of the time, Pallas kernels for 0%

commit v1 on v0

--- a/solution.py
+++ b/solution.py
@@ -1,10 +1,17 @@
+import functools
 import jax
 import jax.numpy as jnp
 from jax import lax
+from jax.experimental import pallas as pl
+from jax.experimental.pallas import tpu as pltpu
 from jax.sharding import PartitionSpec as P
 
-D = 8192
 W = 16
+EPS = 1e-05
+F32 = jnp.float32
+BF16 = jnp.bfloat16
+MESH = pl.DeviceIdType.MESH
+SEGMENTS = 4
 
 
 def rms_scale(values, gain):
@@ -47,7 +54,7 @@
     return result
 
 
-def on_device(
+def on_device_plain(
     resid,
     prefix_values,
     tail_values,
@@ -104,7 +111,7 @@
         preferred_element_type=jnp.float32,
     )
     mixed_squares = lax.psum(jnp.sum(mixed * mixed, axis=1), "ctx")
-    mixed_inverse = lax.rsqrt(mixed_squares / D + 1e-05)
+    mixed_inverse = lax.rsqrt(mixed_squares / norm_gain.shape[0] + 1e-05)
     mlp_gain_own = lax.dynamic_slice_in_dim(mlp_gain, first_col, own_width)
     normed_mlp = (mixed * mixed_inverse[:, None] * mlp_gain_own[None, :]).astype(jnp.bfloat16)
     portion = lax.all_gather(normed_mlp, "ctx", axis=1, tiled=True)
@@ -120,6 +127,600 @@
         tiled=True,
     )
     return total.astype(jnp.bfloat16)
+
+
+def dot(a, b):
+    return jnp.dot(a, b, preferred_element_type=F32)
+
+
+def line_order(z, nz, t):
+    both = jnp.minimum(z, nz - 1 - z)
+    near_step = (t + 1) // 2
+    near_pos = jnp.where(t % 2 == 1, z + near_step, z - near_step)
+    far_pos = jnp.where(2 * z >= nz, z - (t - both), z + (t - both))
+    return jnp.where(t <= 2 * both, near_pos, far_pos)
+
+
+def kernel(
+    n,
+    resid,
+    prefix,
+    tail,
+    tail_lengths,
+    norm_gain,
+    in_weight,
+    skip_gain,
+    residues,
+    rates,
+    out_weight,
+    mlp_gain,
+    gate_weight,
+    up_weight,
+    down_weight,
+    out,
+    w_a,
+    w_b,
+    w_o,
+    g1,
+    g2,
+    acc,
+    ssq,
+    prefix_v,
+    prefix_f,
+    tail_f,
+    taps,
+    conv,
+    st_send,
+    st_recv,
+    mixed,
+    hidden,
+    r1,
+    r2,
+    ru,
+    rd,
+    in_sem,
+    load_sem,
+    down_sem,
+    ag_send,
+    ag_recv,
+    st_ssem,
+    st_rsem,
+    s1,
+    q1,
+    s2,
+    q2,
+    su,
+    qu,
+    sd,
+    qd,
+):
+    nz = n // 4
+    rows, width = resid.shape
+    prompt = prefix.shape[0]
+    branches, slots = tail.shape[0], tail.shape[1]
+    modes = rates.shape[0]
+    total_d = n * width
+    out_rows = rows // n
+    hid = hidden.shape[1]
+    ring = w_o.shape[0] // hid
+    per_step = branches // n
+    me = lax.axis_index("ctx")
+    core = me % 2
+    x = (me // 2) % 2
+    z = me // 4
+    sibling = z * 4 + x * 2 + (1 - core)
+    across = z * 4 + (1 - x) * 2 + core
+    above = me + 4
+    below = me - 4
+    has_above = z < nz - 1
+    has_below = z > 0
+
+    def cols(i):
+        return pl.ds(pl.multiple_of(i * width, width), width)
+
+    def remote(src, dst, ssem, rsem, target):
+        return pltpu.make_async_remote_copy(
+            src_ref=src,
+            dst_ref=dst,
+            send_sem=ssem,
+            recv_sem=rsem,
+            device_id={"ctx": target},
+            device_id_type=MESH,
+        )
+
+    def step_block(m, r):
+        t = m - r % 2
+        valid = (t >= 0) & (t < nz)
+        zt = line_order(z, nz, jnp.clip(t, 0, nz - 1))
+        xx = jnp.where(r % 2 == 0, x, 1 - x)
+        cc = jnp.where(r < 2, core, 1 - core)
+        return valid, zt, zt * 4 + xx * 2 + cc
+
+    def in_load(o):
+        return pltpu.make_async_copy(
+            in_weight.at[:, pl.ds(pl.multiple_of(o * width, width), width), :],
+            w_a.at[:, pl.ds(pl.multiple_of(o * width, width), width), :],
+            in_sem.at[o],
+        )
+
+    resid_load = pltpu.make_async_copy(resid, g1.at[me], load_sem.at[0])
+    prefix_load = pltpu.make_async_copy(prefix, prefix_v, load_sem.at[1])
+    out_load = pltpu.make_async_copy(out_weight, w_o, load_sem.at[2])
+    mlp_loads = [
+        pltpu.make_async_copy(gate_weight.at[:, :width], w_a.at[0], load_sem.at[3]),
+        pltpu.make_async_copy(gate_weight.at[:, width:], w_a.at[1], load_sem.at[4]),
+        pltpu.make_async_copy(up_weight.at[:, :width], w_a.at[2], load_sem.at[5]),
+        pltpu.make_async_copy(up_weight.at[:, width:], w_b, load_sem.at[6]),
+    ]
+
+    def down_load(k):
+        slot = k % ring
+        return pltpu.make_async_copy(
+            down_weight.at[:, cols(k)],
+            w_o.at[pl.ds(pl.multiple_of(slot * hid, hid), hid), :],
+            down_sem.at[slot],
+        )
+
+    resid_load.start()
+    prefix_load.start()
+
+    @pl.loop(0, nz + 1)
+    def _(m):
+        @pl.loop(0, 4)
+        def _(r):
+            valid, _, o = step_block(m, r)
+
+            @pl.when(valid)
+            def _():
+                in_load(o).start()
+
+    out_load.start()
+    mlp_loads[3].start()
+
+    barrier = pltpu.get_barrier_semaphore()
+
+    @pl.loop(1, n)
+    def _(d):
+        pl.semaphore_signal(
+            barrier, inc=1, device_id={"ctx": (me + d) % n}, device_id_type=MESH
+        )
+
+    own_rates = rates[:, cols(me)]
+    own_weights = residues[:, cols(me)] * jnp.sqrt(own_rates)
+    taps[pl.ds(0, W), :] = jnp.zeros((W, width), F32)
+    for first in range(0, slots + W, W):
+        lags = (first + lax.broadcasted_iota(jnp.int32, (W, width), 0)).astype(F32)
+        value = jnp.zeros((W, width), F32)
+        for k in range(modes):
+            value = value + own_weights[k : k + 1] * jnp.exp(-own_rates[k : k + 1] * lags)
+        taps[pl.ds(W + first, W), :] = value
+
+    resid_load.wait()
+    pl.semaphore_wait(barrier, n - 1)
+
+    def gather(index, buf, consume):
+        def copies(o):
+            def to(direction, target):
+                return remote(
+                    buf.at[o],
+                    buf.at[o],
+                    ag_send.at[index * 4 + direction, o],
+                    ag_recv.at[index, o],
+                    target,
+                )
+
+            return to(0, above), to(1, below), to(2, across), to(3, sibling)
+
+        @pl.loop(0, nz + 1)
+        def _(m):
+            @pl.loop(0, 4)
+            def _(r):
+                valid, zt, o = step_block(m, r)
+
+                @pl.when(valid)
+                def _():
+                    up, down, over, side = copies(o)
+
+                    @pl.when(o != me)
+                    def _():
+                        up.wait_recv()
+
+                    @pl.when((r == 0) & (zt <= z) & has_above)
+                    def _():
+                        up.start()
+
+                    @pl.when((r == 0) & (zt >= z) & has_below)
+                    def _():
+                        down.start()
+
+                    @pl.when(r == 0)
+                    def _():
+                        over.start()
+
+                    @pl.when(r < 2)
+                    def _():
+                        side.start()
+
+                    consume(o)
+
+        @pl.loop(0, nz + 1)
+        def _(m):
+            @pl.loop(0, 2)
+            def _(r):
+                valid, zt, o = step_block(m, r)
+
+                @pl.when(valid)
+                def _():
+                    up, down, over, side = copies(o)
+
+                    @pl.when((r == 0) & (zt <= z) & has_above)
+                    def _():
+                        up.wait_send()
+
+                    @pl.when((r == 0) & (zt >= z) & has_below)
+                    def _():
+                        down.wait_send()
+
+                    @pl.when(r == 0)
+                    def _():
+                        over.wait_send()
+
+                    side.wait_send()
+
+    def state_copy(o, source):
+        return remote(
+            st_send.at[o], st_recv.at[source], st_ssem.at[o], st_rsem.at[source], o
+        )
+
+    acc[...] = jnp.zeros_like(acc)
+    ssq[...] = jnp.zeros_like(ssq)
+    prefix_load.wait()
+    last_distance = (n * prompt + slots - (me * prompt + prompt - 1)).astype(F32)
+    seg = prompt // SEGMENTS
+
+    def consume_in(o):
+        in_load(o).wait()
+        at = pl.ds(pl.multiple_of(o * width, width), width)
+        values = g1[o].astype(F32)
+        ssq[...] += jnp.sum(values * values, axis=1, keepdims=True)
+        scaled = (values * norm_gain[:, cols(o)]).astype(BF16)
+        for i in range(3):
+            acc[:, i * width : (i + 1) * width] += dot(scaled, w_a[i, at, :])
+        rate = rates[:, cols(o)]
+        q = jnp.exp(-rate)
+        prefix_f[...] = prefix_v[:, cols(o)].astype(F32)
+
+        def horner(s8, parts):
+            for u in range(8):
+                parts = tuple(
+                    part * q + prefix_f[pl.ds(g * seg + s8 * 8 + u, 1), :]
+                    for g, part in enumerate(parts)
+                )
+            return parts
+
+        zero = jnp.zeros((modes, width), F32)
+        parts = lax.fori_loop(0, seg // 8, horner, (zero,) * SEGMENTS)
+        q_seg = jnp.exp(-rate * float(seg))
+        state = parts[0]
+        for part in parts[1:]:
+            state = state * q_seg + part
+        st_send[o] = state * jnp.exp(-rate * last_distance)
+
+        @pl.when(o != me)
+        def _():
+            state_copy(o, me).start()
+
+        for i in range(per_step):
+            b = o * per_step + i
+            live = lax.broadcasted_iota(jnp.int32, (slots, width), 0) < tail_lengths[b]
+            tail_f[...] = jnp.where(live, tail[b].astype(F32), 0.0)
+            y = jnp.zeros((W, width), F32)
+            for p in range(slots):
+                y = y + taps[pl.ds(W + slots - p, W), :] * tail_f[p : p + 1, :]
+            conv[b] = y
+
+    gather(0, g1, consume_in)
+    for load in mlp_loads[:3]:
+        load.start()
+
+    @pl.loop(1, n)
+    def _(d):
+        source = (me + d) % n
+        state_copy(source, source).wait_recv()
+        state_copy(source, source).wait_send()
+
+    st_recv[me] = st_send[me]
+    states = st_recv[0]
+    for i in range(1, n):
+        states = states + st_recv[i]
+    states = states * own_weights
+    lags = lax.broadcasted_iota(jnp.int32, (W, width), 0).astype(F32)
+    part = jnp.zeros((W, width), F32)
+    for k in range(modes):
+        part = part + states[k : k + 1] * jnp.exp(-own_rates[k : k + 1] * lags)
+    taps[pl.ds(slots + W, W), :] = part
+    ssq[...] = lax.rsqrt(ssq[...] / float(total_d) + EPS)
+    skip = skip_gain[:, cols(me)]
+
+    @pl.loop(0, branches)
+    def _(b):
+        at = pl.ds(pl.multiple_of(b * W, W), W)
+        inverse = ssq[at, :]
+        window = (acc[at, 0:width] * inverse) * (acc[at, 2 * width : 3 * width] * inverse)
+        tail_f[pl.ds(0, W), :] = window
+        y = conv[b] + taps[pl.ds(slots + W, W), :] + skip * window
+        for p in range(W):
+            y = y + taps[pl.ds(W - p, W), :] * tail_f[p : p + 1, :]
+        y = y * (acc[at, width : 2 * width] * inverse)
+        mixed[at, :] = y
+
+    g2[me] = mixed[...].astype(BF16).reshape(g2.shape[1:])
+
+    out_load.wait()
+    mixed[...] = g1[me].astype(F32)
+
+    def consume_out(o):
+        at = pl.ds(pl.multiple_of(o * width, width), width)
+        mixed[...] += dot(g2[o].reshape(rows, width), w_o[at, :])
+
+    gather(1, g2, consume_out)
+    for k in range(ring):
+        down_load(k).start()
+    g1[me] = mixed[...].astype(BF16)
+
+    acc[...] = jnp.zeros_like(acc)
+    ssq[...] = jnp.zeros_like(ssq)
+    for load in mlp_loads:
+        load.wait()
+
+    def consume_mlp(o):
+        at = pl.ds(pl.multiple_of(o * width, width), width)
+        values = g1[o].astype(F32)
+        ssq[...] += jnp.sum(values * values, axis=1, keepdims=True)
+        scaled = (values * mlp_gain[:, cols(o)]).astype(BF16)
+        for i in range(3):
+            acc[:, i * width : (i + 1) * width] += dot(scaled, w_a[i, at, :])
+        acc[:, 3 * width :] += dot(scaled, w_b[at, :])
+
+    gather(2, g1, consume_mlp)
+    ssq[...] = lax.rsqrt(ssq[...] / float(total_d) + EPS)
+
+    @pl.loop(0, rows // 32)
+    def _(i):
+        at = pl.ds(pl.multiple_of(i * 32, 32), 32)
+        inverse = ssq[at, :]
+        gate = acc[at, :hid] * inverse
+        up = acc[at, hid:] * inverse
+        hidden[at, :] = (gate / (1.0 + jnp.exp(-gate)) * up).astype(BF16)
+
+    def core_copy(k):
+        return remote(g2.at[k, :, :, 1 - core], r1.at[k], s1.at[k], q1.at[k], sibling)
+
+    def across_copy(k):
+        return remote(g2.at[k, :, 1 - x, core], r2.at[k], s2.at[k], q2.at[k], across)
+
+    def up_copy(k, d):
+        return remote(
+            g2.at[k, d, x, core], ru.at[k, d], su.at[k, d], qu.at[k, d], above
+        )
+
+    def down_copy(k, d):
+        return remote(
+            g2.at[k, d, x, core], rd.at[k, d], sd.at[k, d], qd.at[k, d], below
+        )
+
+    def add_into(k, d, arrived):
+        g2[k, d, x, core] = (
+            g2[k, d, x, core].astype(F32) + arrived.astype(F32)
+        ).astype(BF16)
+
+    def stage(k, body):
+        @pl.when((k >= 0) & (k < n))
+        def _():
+            body(k)
+
+    def multiply(k):
+        down_load(k).wait()
+        slot = k % ring
+        at = pl.ds(pl.multiple_of(slot * hid, hid), hid)
+        own = jnp.where(k == me, 1.0, 0.0).astype(F32)
+        product = dot(hidden[...], w_o[at, :]) + own * mixed[...]
+        g2[k] = product.astype(BF16).reshape(g2.shape[1:])
+        core_copy(k).start()
+
+        @pl.when(k + ring < n)
+        def _():
+            down_load(k + ring).start()
+
+    def sum_cores(k):
+        core_copy(k).wait_recv()
+        for d in range(nz):
+            for xx in range(2):
+                g2[k, d, xx, core] = (
+                    g2[k, d, xx, core].astype(F32) + r1[k, d, xx].astype(F32)
+                ).astype(BF16)
+        across_copy(k).start()
+
+    def sum_across(k):
+        across_copy(k).wait_recv()
+        for d in range(nz):
+            add_into(k, d, r2[k, d])
+
+    def send_up(k):
+        for d in range(1, nz):
+
+            @pl.when((z < d) & has_below)
+            def _():
+                up_copy(k, d).wait_recv()
+                add_into(k, d, ru[k, d])
+
+            @pl.when(z < d)
+            def _():
+                up_copy(k, d).start()
+
+    def send_down(k):
+        for d in range(nz - 1):
+
+            @pl.when((z > d) & has_above)
+            def _():
+                down_copy(k, d).wait_recv()
+                add_into(k, d, rd[k, d])
+
+            @pl.when(z > d)
+            def _():
+                down_copy(k, d).start()
+
+    def finish(k):
+        @pl.when(has_below)
+        def _():
+            up_copy(k, z).wait_recv()
+            add_into(k, z, ru[k, z])
+
+        @pl.when(has_above)
+        def _():
+            down_copy(k, z).wait_recv()
+            add_into(k, z, rd[k, z])
+
+        out[:, cols(k)] = g2[k, z, x, core]
+
+    @pl.loop(0, n + nz + 3)
+    def _(i):
+        stage(i, multiply)
+        stage(i - 1, sum_cores)
+        stage(i - 2, sum_across)
+        stage(i - 2 - z, send_up)
+        stage(i - 2 - (nz - 1 - z), send_down)
+        stage(i - 2 - nz, finish)
+
+    @pl.loop(0, n)
+    def _(k):
+        core_copy(k).wait_send()
+        across_copy(k).wait_send()
+        for d in range(1, nz):
+
+            @pl.when(z < d)
+            def _():
+                up_copy(k, d).wait_send()
+
+        for d in range(nz - 1):
+
+            @pl.when(z > d)
+            def _():
+                down_copy(k, d).wait_send()
+
+
+def on_device_kernel(*args):
+    n = lax.axis_size("ctx")
+    (resid, prefix, tail, lengths, norm_gain, in_weight, skip_gain, residues, rates) = args[:9]
+    (out_weight, mlp_gain, gate_weight, up_weight, down_weight) = args[9:]
+    rows, width = resid.shape
+    hid = down_weight.shape[0]
+    total = n * width
+    modes = rates.shape[0]
+    nz = n // 4
+    slots = tail.shape[1]
+    prompt = prefix.shape[0]
+    out_rows = rows // n
+    dma = pltpu.SemaphoreType.DMA
+    vmem = pl.BlockSpec(memory_space=pltpu.VMEM)
+    hbm = pl.BlockSpec(memory_space=pl.ANY)
+    smem = pl.BlockSpec(memory_space=pltpu.SMEM)
+    flops = 2 * rows * (3 * total * width + total * width + 3 * total * hid)
+    return pl.pallas_call(
+        functools.partial(kernel, n),
+        out_shape=jax.ShapeDtypeStruct((out_rows, total), BF16),
+        in_specs=[
+            hbm, hbm, vmem, smem, vmem, hbm, vmem, vmem, vmem, hbm, vmem, hbm, hbm, hbm,
+        ],
+        out_specs=vmem,
+        scratch_shapes=[
+            pltpu.VMEM((3, total, width), BF16),
+            pltpu.VMEM((total, width), BF16),
+            pltpu.VMEM((total, width), BF16),
+            pltpu.VMEM((n, rows, width), BF16),
+            pltpu.VMEM((n, nz, 2, 2, out_rows, width), BF16),
+            pltpu.VMEM((rows, 4 * width), F32),
+            pltpu.VMEM((rows, 1), F32),
+            pltpu.VMEM((prompt, total), BF16),
+            pltpu.VMEM((prompt, width), F32),
+            pltpu.VMEM((slots, width), F32),
+            pltpu.VMEM((slots + 2 * W, width), F32),
+            pltpu.VMEM((tail.shape[0], W, width), F32),
+            pltpu.VMEM((n, modes, width), F32),
+            pltpu.VMEM((n, modes, width), F32),
+            pltpu.VMEM((rows, width), F32),
+            pltpu.VMEM((rows, hid), BF16),
+            pltpu.VMEM((n, nz, 2, out_rows, width), BF16),
+            pltpu.VMEM((n, nz, out_rows, width), BF16),
+            pltpu.VMEM((n, nz, out_rows, width), BF16),
+            pltpu.VMEM((n, nz, out_rows, width), BF16),
+            dma((n,)),
+            dma((7,)),
+            dma((total // hid,)),
+            dma((12, n)),
+            dma((3, n)),
+            dma((n,)),
+            dma((n,)),
+            dma((n,)),
+            dma((n,)),
+            dma((n,)),
+            dma((n,)),
+            dma((n, nz)),
+            dma((n, nz)),
+            dma((n, nz)),
+            dma((n, nz)),
+        ],
+        compiler_params=pltpu.CompilerParams(
+            collective_id=0,
+            has_side_effects=True,
+            vmem_limit_bytes=63 * 1024 * 1024,
+        ),
+        cost_estimate=pl.CostEstimate(
+            flops=flops, bytes_accessed=flops // rows, transcendentals=0
+        ),
+    )(
+        resid,
+        prefix,
+        tail,
+        lengths,
+        norm_gain[None, :],
+        in_weight,
+        skip_gain[None, :],
+        residues,
+        rates,
+        out_weight,
+        mlp_gain[None, :],
+        gate_weight,
+        up_weight,
+        down_weight,
+    )
+
+
+def fits_kernel(args):
+    n = lax.axis_size("ctx")
+    rows, width = args[0].shape
+    hid, total = args[13].shape
+    branches, slots = args[2].shape[:2]
+    prompt = args[1].shape[0]
+    return (
+        n % 4 == 0
+        and n >= 8
+        and width % 128 == 0
+        and rows % n == 0
+        and (rows // n) % 16 == 0
+        and hid == 2 * width
+        and (total // hid) <= n
+        and branches % n == 0
+        and slots % 16 == 0
+        and slots >= W
+        and prompt % (8 * SEGMENTS) == 0
+    )
+
+
+def on_device(*args):
+    if fits_kernel(args):
+        return on_device_kernel(*args)
+    return on_device_plain(*args)
 
 
 def solution(mesh):

time: 455 us -> 177 us (0.39)
  waiting for transfers between devices: 306 us -> 0 us
  Pallas kernels: 0 us -> 175 us
  matrix products: 67.4 us -> 0 us
  blocking collectives: 30.9 us -> 0 us
  other arithmetic: 23.5 us -> 0 us
  between operations: 13.3 us -> 0.01 us
  local copies, waits for them, and re-layouts: 13.1 us -> 1.67 us
    pallas_call x0 -> x1, Pallas kernels: none -> 175 us  [on_device_kernel(): pl.pallas_call(functools.partial(kernel, n), out_shape=jax.ShapeDtypeStru...]
    reduce_scatter x2 -> x0, waiting for transfers between devices: 154 us -> none  [the longest x1 103 us: on_device(): lax.psum_scatter(lax.dynamic_update_slice_in_dim(product, own_cols, first...]
    all_gather x3 -> x0, waiting for transfers between devices: 151 us -> none  [the longest x1 50.5 us: on_device(): lax.all_gather(mixer_in, 'ctx', axis=1, tiled=True)]
    dot_general x8 -> x0, matrix products: 67.4 us -> none  [the longest x1 23.9 us: on_device(): product = jnp.dot(hidden, down_weight, preferred_element_type=jnp.float32)]
    psum x1 -> x0, blocking collectives: 30.9 us -> none  [on_device(): mixed_squares = lax.psum(jnp.sum(mixed * mixed, axis=1), 'ctx')]
    reduce_sum x2 -> x0, other arithmetic: 10.9 us -> none  [the longest x1 7.63 us: mode_states(): jnp.sum(jnp.exp(-rates[mode][None, :] * distance[:, None]) * values, axis=0)]
    dot_general x2 -> x0, local copies, waits for them, and re-layouts: 5.63 us -> none  [the longest x1 2.84 us: lag_toeplitz(): return jnp.einsum('jpn,nc->jpc', picked.astype(jnp.float32), near_taps)]
  transfers between devices with their start and end apart: 5 -> 0, of which waited for: 5 -> 0; matrix products, arithmetic and copies ran while one was open for 2% -> 0% of each run, Pallas kernels for 0% -> 0%
where the time goes in v1:
time: 177 us
  Pallas kernels  175 us (99%)
    pallas_call x1, Pallas kernels, on_device_kernel(): pl.pallas_call(functools.partial(kernel, n), out_shape=jax.ShapeDtypeStru...  175 us

profile of v1, /device:TPU:0, one launch (start us, length us, event | category | flops | bytes accessed | tf_op | source)
XLA Modules:
  0.0 177.1 jit_solution(2493619050774636575)
XLA Ops:
  0.0 175.5 %shard_map.136 = bf16[16,8192]{1,0:T(8,128)(2,1)} custom-call(bf16[256,512]{1,0:T(8,128)(2,1)} %resid.1, bf16[128,8192]{1,0:T(8,128)(2,1)} %prefix.1, bf16[16,48,512]{2,1,0:T(8,128)(2,1)} %tail.1, s32[16]{0:T(128)} %tail_lengths.1, f32[1,8192]{1,0:T(1,128)} %bitcast.3, bf16[3,8192,512]{2,1,0:T(8,128)(2,1)} %in_weight.1, f32[1,8192]{1,0:T(1,128)} %bitcast.4, ...), custom_call_target="tpu_custom_call" | custom-call | flops 21474836480 | bytes 83886080 | tf_op jit(solution)/shard_map/pallas_call | solution.py:629
  175.5 1.7 copy.16

commit v2 on v1

--- a/solution.py
+++ b/solution.py
@@ -136,7 +136,7 @@
 def line_order(z, nz, t):
     both = jnp.minimum(z, nz - 1 - z)
     near_step = (t + 1) // 2
-    near_pos = jnp.where(t % 2 == 1, z + near_step, z - near_step)
+    near_pos = jnp.where(t % 2 == 1, z - near_step, z + near_step)
     far_pos = jnp.where(2 * z >= nz, z - (t - both), z + (t - both))
     return jnp.where(t <= 2 * both, near_pos, far_pos)
 
@@ -177,7 +177,6 @@
     r1,
     r2,
     ru,
-    rd,
     in_sem,
     load_sem,
     down_sem,
@@ -191,8 +190,6 @@
     q2,
     su,
     qu,
-    sd,
-    qd,
 ):
     nz = n // 4
     rows, width = resid.shape
@@ -229,11 +226,16 @@
         )
 
     def step_block(m, r):
-        t = m - r % 2
-        valid = (t >= 0) & (t < nz)
-        zt = line_order(z, nz, jnp.clip(t, 0, nz - 1))
-        xx = jnp.where(r % 2 == 0, x, 1 - x)
-        cc = jnp.where(r < 2, core, 1 - core)
+        kind = r % 3
+        t = jnp.maximum(m - 1, 0)
+        zt = jnp.where(
+            kind == 0, z - m, jnp.where(kind == 1, z + m, line_order(z, nz, t))
+        )
+        valid = jnp.where(kind == 1, m > 0, (kind == 0) | (m > 0))
+        valid = valid & (zt >= 0) & (zt < nz)
+        zt = jnp.clip(zt, 0, nz - 1)
+        xx = jnp.where(kind < 2, x, 1 - x)
+        cc = jnp.where(r < 3, core, 1 - core)
         return valid, zt, zt * 4 + xx * 2 + cc
 
     def in_load(o):
@@ -264,9 +266,8 @@
     resid_load.start()
     prefix_load.start()
 
-    @pl.loop(0, nz + 1)
-    def _(m):
-        @pl.loop(0, 4)
+    def start_loads(m):
+        @pl.loop(0, 6)
         def _(r):
             valid, _, o = step_block(m, r)
 
@@ -274,8 +275,15 @@
             def _():
                 in_load(o).start()
 
-    out_load.start()
-    mlp_loads[3].start()
+    def load_ahead(m):
+        @pl.when(m < nz)
+        def _():
+            start_loads(m + 1)
+
+        @pl.when(m == nz - 1)
+        def _():
+            out_load.start()
+            mlp_loads[3].start()
 
     barrier = pltpu.get_barrier_semaphore()
 
@@ -297,8 +305,9 @@
 
     resid_load.wait()
     pl.semaphore_wait(barrier, n - 1)
-
-    def gather(index, buf, consume):
+    start_loads(0)
+
+    def gather(index, buf, consume, ahead=None):
         def copies(o):
             def to(direction, target):
                 return remote(
@@ -313,9 +322,11 @@
 
         @pl.loop(0, nz + 1)
         def _(m):
-            @pl.loop(0, 4)
+            @pl.loop(0, 6)
             def _(r):
                 valid, zt, o = step_block(m, r)
+                if ahead is not None:
+                    pl.when(r == 3)(lambda: ahead(m))
 
                 @pl.when(valid)
                 def _():
@@ -325,19 +336,19 @@
                     def _():
                         up.wait_recv()
 
-                    @pl.when((r == 0) & (zt <= z) & has_above)
+                    @pl.when((r < 2) & (zt <= z) & has_above)
                     def _():
                         up.start()
 
-                    @pl.when((r == 0) & (zt >= z) & has_below)
+                    @pl.when((r < 2) & (zt >= z) & has_below)
                     def _():
                         down.start()
 
-                    @pl.when(r == 0)
+                    @pl.when(r < 2)
                     def _():
                         over.start()
 
-                    @pl.when(r < 2)
+                    @pl.when(r < 3)
                     def _():
                         side.start()
 
@@ -345,7 +356,7 @@
 
         @pl.loop(0, nz + 1)
         def _(m):
-            @pl.loop(0, 2)
+            @pl.loop(0, 3)
             def _(r):
                 valid, zt, o = step_block(m, r)
 
@@ -353,15 +364,15 @@
                 def _():
                     up, down, over, side = copies(o)
 
-                    @pl.when((r == 0) & (zt <= z) & has_above)
+                    @pl.when((r < 2) & (zt <= z) & has_above)
                     def _():
                         up.wait_send()
 
-                    @pl.when((r == 0) & (zt >= z) & has_below)
+                    @pl.when((r < 2) & (zt >= z) & has_below)
                     def _():
                         down.wait_send()
 
-                    @pl.when(r == 0)
+                    @pl.when(r < 2)
                     def _():
                         over.wait_send()
 
@@ -419,7 +430,7 @@
                 y = y + taps[pl.ds(W + slots - p, W), :] * tail_f[p : p + 1, :]
             conv[b] = y
 
-    gather(0, g1, consume_in)
+    gather(0, g1, consume_in, load_ahead)
     for load in mlp_loads[:3]:
         load.start()
 
@@ -499,14 +510,13 @@
     def across_copy(k):
         return remote(g2.at[k, :, 1 - x, core], r2.at[k], s2.at[k], q2.at[k], across)
 
-    def up_copy(k, d):
+    def line_copy(k, d, source):
         return remote(
-            g2.at[k, d, x, core], ru.at[k, d], su.at[k, d], qu.at[k, d], above
-        )
-
-    def down_copy(k, d):
-        return remote(
-            g2.at[k, d, x, core], rd.at[k, d], sd.at[k, d], qd.at[k, d], below
+            g2.at[k, d, x, core],
+            ru.at[k, source],
+            su.at[k, d],
+            qu.at[k, source],
+            d * 4 + x * 2 + core,
         )
 
     def add_into(k, d, arrived):
@@ -545,68 +555,41 @@
         across_copy(k).wait_recv()
         for d in range(nz):
             add_into(k, d, r2[k, d])
-
-    def send_up(k):
+        for d in range(nz):
+
+            @pl.when(z != d)
+            def _():
+                line_copy(k, d, z).start()
+
+    def finish(k):
+        ru[k, z] = g2[k, z, x, core]
+        for d in range(nz):
+
+            @pl.when(z != d)
+            def _():
+                line_copy(k, d, d).wait_recv()
+
+        value = ru[k, 0].astype(F32)
         for d in range(1, nz):
-
-            @pl.when((z < d) & has_below)
-            def _():
-                up_copy(k, d).wait_recv()
-                add_into(k, d, ru[k, d])
-
-            @pl.when(z < d)
-            def _():
-                up_copy(k, d).start()
-
-    def send_down(k):
-        for d in range(nz - 1):
-
-            @pl.when((z > d) & has_above)
-            def _():
-                down_copy(k, d).wait_recv()
-                add_into(k, d, rd[k, d])
-
-            @pl.when(z > d)
-            def _():
-                down_copy(k, d).start()
-
-    def finish(k):
-        @pl.when(has_below)
-        def _():
-            up_copy(k, z).wait_recv()
-            add_into(k, z, ru[k, z])
-
-        @pl.when(has_above)
-        def _():
-            down_copy(k, z).wait_recv()
-            add_into(k, z, rd[k, z])
-
-        out[:, cols(k)] = g2[k, z, x, core]
-
-    @pl.loop(0, n + nz + 3)
+            value = value + ru[k, d].astype(F32)
+        out[:, cols(k)] = value.astype(BF16)
+
+    @pl.loop(0, n + 6)
     def _(i):
         stage(i, multiply)
+        stage(i - 3, sum_across)
         stage(i - 1, sum_cores)
-        stage(i - 2, sum_across)
-        stage(i - 2 - z, send_up)
-        stage(i - 2 - (nz - 1 - z), send_down)
-        stage(i - 2 - nz, finish)
+        stage(i - 6, finish)
 
     @pl.loop(0, n)
     def _(k):
         core_copy(k).wait_send()
         across_copy(k).wait_send()
-        for d in range(1, nz):
-
-            @pl.when(z < d)
+        for d in range(nz):
+
+            @pl.when(z != d)
             def _():
-                up_copy(k, d).wait_send()
-
-        for d in range(nz - 1):
-
-            @pl.when(z > d)
-            def _():
-                down_copy(k, d).wait_send()
+                line_copy(k, d, z).wait_send()
 
 
 def on_device_kernel(*args):
@@ -653,7 +636,6 @@
             pltpu.VMEM((n, nz, 2, out_rows, width), BF16),
             pltpu.VMEM((n, nz, out_rows, width), BF16),
             pltpu.VMEM((n, nz, out_rows, width), BF16),
-            pltpu.VMEM((n, nz, out_rows, width), BF16),
             dma((n,)),
             dma((7,)),
             dma((total // hid,)),
@@ -665,8 +647,6 @@
             dma((n,)),
             dma((n,)),
             dma((n,)),
-            dma((n, nz)),
-            dma((n, nz)),
             dma((n, nz)),
             dma((n, nz)),
         ],

time: 177 us -> 149 us (0.84)
  Pallas kernels: 175 us -> 147 us
    pallas_call x1, Pallas kernels: 175 us -> 147 us  [on_device_kernel(): pl.pallas_call(functools.partial(kernel, n), out_shape=jax.ShapeDtypeStru...]
where the time goes in v2:
time: 149 us
  Pallas kernels  147 us (99%)
  local copies, waits for them, and re-layouts  1.67 us (1%)
    pallas_call x1, Pallas kernels, on_device_kernel(): pl.pallas_call(functools.partial(kernel, n), out_shape=jax.ShapeDtypeStru...  147 us

profile of v2, /device:TPU:0, one launch (start us, length us, event | category | flops | bytes accessed | tf_op | source)
XLA Modules:
  0.0 148.6 jit_solution(14875475759122168586)
XLA Ops:
  0.0 147.0 %shard_map.136 = bf16[16,8192]{1,0:T(8,128)(2,1)} custom-call(bf16[256,512]{1,0:T(8,128)(2,1)} %resid.1, bf16[128,8192]{1,0:T(8,128)(2,1)} %prefix.1, bf16[16,48,512]{2,1,0:T(8,128)(2,1)} %tail.1, s32[16]{0:T(128)} %tail_lengths.1, f32[1,8192]{1,0:T(1,128)} %bitcast.3, bf16[3,8192,512]{2,1,0:T(8,128)(2,1)} %in_weight.1, f32[1,8192]{1,0:T(1,128)} %bitcast.4, ...), custom_call_target="tpu_custom_call" | custom-call | flops 21474836480 | bytes 83886080 | tf_op jit(solution)/shard_map/pallas_call | solution.py:612
  147.0 1.7 %copy.16 = bf16[16,8192]{1,0:T(8,128)(2,1)} copy(bf16[16,8192]{1,0:T(8,128)(2,1)} %shard_map.136) | data formatting | bytes 524288
